TPU v7x, 32 devices: a whole 2x2x4 slice. The times are simulated.
32 devices in a mesh: scan: 8 (over z, x), tile: 4 (over y, core).
Axes of the slice: x: 2, y: 2, z: 4, core: 2. Of those that a mesh axis runs over, the one named last changes fastest.
Arguments:
- probe_modes: float32 [3072, 256], P(('scan', 'tile')), may hold values from -2.1 to 2.1
- object_tiles: float32 [4, 2, 2, 320, 320], P('tile'), may hold values from -4 to 4
- scan_offsets: int32 [64, 2], P(('scan', 'tile')), may hold values from 0 to 64, as said below
- patch_tiles: int32 [64], P(('scan', 'tile')), may hold values from 0 to 3, as said below
- amplitudes: bfloat16 [64, 256, 256], P(('scan', 'tile')), may hold values from 0.5 to 20
Outputs:
- probe_gradient: float32 [3072, 256], P(('scan', 'tile'))
- object_gradient: float32 [4, 2, 2, 320, 320], P('tile', None, None, 'scan')
Inputs may be any that keep to these rules, and one draw needn't show every extreme that they name: `patch_tiles`: each entry names the tile that wholly holds the patch of its position. `scan_offsets`: every patch lies wholly inside its tile.
All inputs are finite; a program needn't handle non-finite values.
Results may differ from a plain program's by a relative error of at most 0.02.
Values sent between devices are 32-bit elements; how exact they have to be, the bound alone decides.
A program may use at most 128 MiB of HBM per device.

v0:
```python
import math

import jax
import jax.numpy as jnp
from jax import lax
from jax.sharding import PartitionSpec as P


def complex_tables(pixels):
    pixel_index = jnp.arange(pixels, dtype=jnp.int32)
    offset = pixel_index[:, None] - pixel_index[None, :]
    chirp_phase = (offset * offset % (2 * pixels)).astype(jnp.float32) * (math.pi / pixels)
    product = (pixel_index[:, None] * pixel_index[None, :] % pixels).astype(jnp.float32) * (
        2.0 * math.pi / pixels
    )
    norm_scale = 1.0 / math.sqrt(pixels)
    fresnel = (jnp.stack([jnp.cos(chirp_phase), jnp.sin(chirp_phase)]) * norm_scale).astype(
        jnp.bfloat16
    )
    spectral = (jnp.stack([jnp.cos(product), -jnp.sin(product)]) * norm_scale).astype(jnp.bfloat16)
    return (fresnel, spectral)


def multiply_object(exit_wave, object_patch):
    real_part = exit_wave[0] * object_patch[0] - exit_wave[1] * object_patch[1]
    imag_part = exit_wave[0] * object_patch[1] + exit_wave[1] * object_patch[0]
    return jnp.stack([real_part, imag_part])


def left_side(matrix_part, component):
    return jnp.einsum("ij,mjk->mik", matrix_part, component, preferred_element_type=jnp.float32)


def right_side(component, matrix_part):
    return jnp.einsum("mik,jk->mij", component, matrix_part, preferred_element_type=jnp.float32)


def left_product(matrix, exit_wave):
    real_part = left_side(matrix[0], exit_wave[0]) - left_side(matrix[1], exit_wave[1])
    imag_part = left_side(matrix[0], exit_wave[1]) + left_side(matrix[1], exit_wave[0])
    return jnp.stack([real_part, imag_part])


def right_product(exit_wave, matrix):
    real_part = right_side(exit_wave[0], matrix[0]) - right_side(exit_wave[1], matrix[1])
    imag_part = right_side(exit_wave[0], matrix[1]) + right_side(exit_wave[1], matrix[0])
    return jnp.stack([real_part, imag_part])


def position_loss(probe_values, patch_values, amplitude, fresnel, spectral):
    exit_wave = probe_values
    layers = patch_values.shape[0]
    for slice_index in range(layers):
        exit_wave = multiply_object(exit_wave, patch_values[slice_index])
        matrix = fresnel if slice_index < layers - 1 else spectral
        rounded = exit_wave.astype(jnp.bfloat16)
        halfway = left_product(matrix, rounded).astype(jnp.bfloat16)
        exit_wave = right_product(halfway, matrix)
    intensity = jnp.sum(exit_wave * exit_wave, axis=(0, 1))
    residue = jnp.sqrt(intensity + 1.0) - amplitude.astype(jnp.float32)
    return jnp.sum(residue * residue)


def body(probe_modes, object_tiles, scan_offsets, patch_tiles, amplitudes):
    tile_count = lax.axis_size("tile")
    scan_count = lax.axis_size("scan")
    pixels = probe_modes.shape[1]
    layers = object_tiles.shape[1]
    side = object_tiles.shape[3]
    whole_probe = lax.all_gather(probe_modes, ("scan", "tile"), axis=0, tiled=True)
    probe_field = whole_probe.reshape(2, -1, pixels, pixels)
    fresnel, spectral = complex_tables(pixels)
    whole_object = lax.all_gather(object_tiles, "tile", axis=0, tiled=True)

    def cut_own(tile_number, corner):
        anchor = (tile_number, jnp.int32(0), jnp.int32(0), corner[0], corner[1])
        return lax.dynamic_slice(whole_object, anchor, (1, layers, 2, pixels, pixels))[0]

    own_patches = jax.vmap(cut_own)(patch_tiles, scan_offsets)

    def one_position(probe_total, inputs):
        object_patch, amplitude = inputs

        def local_loss(probe_values, patch_values):
            return position_loss(probe_values, patch_values, amplitude, fresnel, spectral)

        misfit, pullback = jax.vjp(local_loss, probe_field, object_patch)
        probe_part, patch_part = pullback(jnp.ones_like(misfit))
        return (probe_total + probe_part, patch_part)

    probe_total, patch_gradients = lax.scan(
        one_position, jnp.zeros_like(probe_field), (own_patches, amplitudes)
    )

    def add_patch(object_total, inputs):
        gradient_piece, tile_number, corner = inputs
        anchor = (tile_number, jnp.int32(0), jnp.int32(0), corner[0], corner[1])
        current = lax.dynamic_slice(object_total, anchor, (1,) + gradient_piece.shape)
        return (
            lax.dynamic_update_slice(object_total, current + gradient_piece[None], anchor),
            None,
        )

    whole_shape = (tile_count,) + object_tiles.shape[1:]
    object_total, _ = lax.scan(
        add_patch, jnp.zeros(whole_shape, jnp.float32), (patch_gradients, patch_tiles, scan_offsets)
    )
    row_count = side // scan_count
    arranged = object_total.reshape(tile_count, layers, 2, scan_count, row_count, side)
    arranged = arranged.transpose(3, 0, 1, 2, 4, 5).reshape(
        scan_count * tile_count, layers, 2, row_count, side
    )
    object_gradient = lax.psum_scatter(arranged, ("scan", "tile"), scatter_dimension=0, tiled=True)
    probe_gradient = lax.psum_scatter(
        probe_total.reshape(-1, pixels), ("scan", "tile"), scatter_dimension=0, tiled=True
    )
    return (probe_gradient, object_gradient)


def solution(mesh):
    placed = (
        P(("scan", "tile"), None),
        P("tile", None, None, None, None),
        P(("scan", "tile"), None),
        P(("scan", "tile")),
        P(("scan", "tile"), None, None),
    )
    return jax.shard_map(
        body,
        mesh=mesh,
        in_specs=placed,
        out_specs=(P(("scan", "tile"), None), P("tile", None, None, "scan", None)),
        check_vma=False,
    )
```

profile of v0, /device:TPU:0, one launch (start us, length us, event | category | flops | bytes accessed | tf_op | source)
XLA Modules:
  0.0 476.8 jit_solution(3388957440952484923)
XLA Ops:
  8.9 1.0 fusion.183
  10.0 0.7 fusion.172
  10.7 1.0 sine_negate_fusion
  12.0 60.7 %all-gather.3.cloned.1.call-done = f32[3072,256]{1,0:T(8,128)} async-done(((f32[96,256]{1,0:T(8,128)}), f32[3072,256]{1,0:T(8,128)}) %all-gather.3.cloned.1.call-update) | async-done | bytes 3145744 | tf_op jit(solution)/shard_map/all_gather | solution.py:70
  72.7 2.4 copy.128
  75.1 53.4 %all-gather.5.cloned.1.call-done = f32[4,2,2,320,320]{4,3,2,1,0:T(8,128)} async-done(((f32[1,2,2,320,320]{4,3,2,1,0:T(8,128)}), f32[4,2,2,320,320]{4,3,2,1,0:T(8,128)}) %all-gather.5.cloned.1.call-update) | async-done | bytes 6553616 | tf_op jit(solution)/shard_map/all_gather | solution.py:73
  128.4 10.6 %while.25 = (s32[]{:T(128)}, f32[4,2,2,320,320]{4,3,2,1,0:T(8,128)}, s32[2,5]{1,0:T(2,128)S(1)}, f32[2,1,2,2,256,256]{5,4,3,2,1,0:T(8,128)}, s32[]{:T(128)}) while((s32[]{:T(128)}, f32[4,2,2,320,320]{4,3,2,1,0:T(8,128)}, s32[2,5]{1,0:T(2,128)S(1)}, f32[2,1,2,2,256,256]{5,4,3,2,1,0:T(8,128)}, s32[]{:T(128)}) %tuple.102), condition=%wide.while_cond, body=%wide.while_body.sunk | while | flops 2 | bytes 2099329 | solution.py:77
  129.1 4.7 bitcast_dynamic-update-slice_fusion.4
  134.4 4.7 bitcast_dynamic-update-slice_fusion.4
  139.1 98.4 %while.26 = (s32[]{:T(128)}, f32[2,6,256,256]{2,3,1,0:T(8,128)}, f32[2,2,2,256,256]{4,3,2,1,0:T(8,128)}, f32[2,6,256,256]{2,3,1,0:T(8,128)S(1)}, f32[2,2,2,256,2...) while((s32[]{:T(128)}, f32[2,6,256,256]{2,3,1,0:T(8,128)}, ...), condition=%wide.region_10.11_spmd.clone, body=%wide.region_0.10_spmd.clone.sunk | while | flops 6493634560 | bytes 218235760 | solution.py:91
  139.1 3.0 dynamic-slice_bitcast_fusion.5
  142.0 1.8 copy.161
  143.8 1.8 copy.162
  145.6 1.5 fusion.351
  159.7 1.6 fusion.382
  166.1 3.5 fusion.381
  169.7 1.8 copy.163
  171.5 1.8 copy.164
  173.3 1.8 copy.165
  175.0 1.8 copy.166
  176.8 1.6 add_bitcast_fusion.6
  178.5 1.1 bitcast_dynamic-update-slice_fusion.5
  179.6 2.8 slice_multiply_fusion.9
  182.5 5.4 %select_add_fusion.2 = f32[2,6,256,256]{2,3,1,0:T(8,128)} fusion(f32[2,6,256,256]{2,3,1,0:T(8,128)} %get-tuple-element.413, f32[1,6,256,256]{2,3,1,0:T(8,128)} %get-tuple-element.371, f32[1,6,256,256]{2,3,1,0:T(8,128)} %get-tuple-element.372, f32[1,6,256,256]{2,3,1,0:T(8,128)} %get-tuple-element.373, f32[1,6,256,256]{2,3,1,0:T(8,128)} %get-tuple-element.374, ...), kind=kLoop, calls=%fused_computation.5.clone.1 | loop fusion | flops 3932160 | bytes 12582913 | tf_op jit(solution)/shard_map/while/body/eval_jaxpr/add | solution.py:89
  187.8 3.0 dynamic-slice_bitcast_fusion.5
  190.8 1.8 copy.161
  192.6 1.8 copy.162
  194.3 1.5 fusion.351
  208.5 1.6 fusion.382
  214.9 3.5 fusion.381
  218.5 1.8 copy.163
  220.3 1.8 copy.164
  222.0 1.8 copy.165
  223.8 1.8 copy.166
  225.6 1.6 add_bitcast_fusion.6
  227.3 1.1 bitcast_dynamic-update-slice_fusion.5
  228.4 2.8 slice_multiply_fusion.9
  231.2 6.3 %select_add_fusion.2 = f32[2,6,256,256]{2,3,1,0:T(8,128)} fusion(f32[2,6,256,256]{2,3,1,0:T(8,128)} %get-tuple-element.413, f32[1,6,256,256]{2,3,1,0:T(8,128)} %get-tuple-element.371, f32[1,6,256,256]{2,3,1,0:T(8,128)} %get-tuple-element.372, f32[1,6,256,256]{2,3,1,0:T(8,128)} %get-tuple-element.373, f32[1,6,256,256]{2,3,1,0:T(8,128)} %get-tuple-element.374, ...), kind=kLoop, calls=%fused_computation.5.clone.1 | loop fusion | flops 3932160 | bytes 12582913 | tf_op jit(solution)/shard_map/while/body/eval_jaxpr/add | solution.py:89
  237.5 3.6 copy.129
  241.2 4.0 broadcast_in_dim.99
  245.1 40.2 %while.24 = (s32[]{:T(128)}, f32[4,2,2,320,320]{4,3,2,1,0:T(8,128)}, s32[2]{0:T(128)S(1)}, s32[2,2]{1,0:T(2,128)S(1)}, f32[2,2,2,256,256]{4,3,2,1,0:T(8,128)}, /*index=5*/s32[]{:T(128)}, s32[]{:T(128)}, s32[]{:T(128)}, s32[]{:T(128)}) while((s32[]{:T(128)}, f32[4,2,2,320,320]{4,3,2,1,0:T(8,128)}, s32[2]{0:T(128)S(1)}, ...), condition=%wide.region_13.14_spmd, body=%wide.region_12.13_spmd.sunk | while | flops 262155 | bytes 5243143 | solution.py:105
  251.7 2.1 dynamic-slice_add_fusion.2
  253.9 11.3 %dynamic_update_slice.11 = f32[4,2,2,320,320]{4,3,2,1,0:T(8,128)} dynamic-update-slice(f32[4,2,2,320,320]{4,3,2,1,0:T(8,128)} %get-tuple-element.444, f32[1,2,2,256,256]{4,3,2,1,0:T(8,128)S(1)} %dynamic-slice_add_fusion.2, s32[]{:T(128)S(6)} %select_n.91, s32[]{:T(128)} %constant.64.clone.1..sunk, s32[]{:T(128)} %constant.64.clone.1..sunk, s32[]{:T(128)S(6)} %select_n.92, s32[]{:T(128)S(6)} %select_n.93) | dynamic-update-slice | bytes 2097156 | tf_op jit(solution)/shard_map/while/body/eval_jaxpr/dynamic_update_slice | solution.py:100
  271.8 2.1 dynamic-slice_add_fusion.2
  274.0 11.4 %dynamic_update_slice.11 = f32[4,2,2,320,320]{4,3,2,1,0:T(8,128)} dynamic-update-slice(f32[4,2,2,320,320]{4,3,2,1,0:T(8,128)} %get-tuple-element.444, f32[1,2,2,256,256]{4,3,2,1,0:T(8,128)S(1)} %dynamic-slice_add_fusion.2, s32[]{:T(128)S(6)} %select_n.91, s32[]{:T(128)} %constant.64.clone.1..sunk, s32[]{:T(128)} %constant.64.clone.1..sunk, s32[]{:T(128)S(6)} %select_n.92, s32[]{:T(128)S(6)} %select_n.93) | dynamic-update-slice | bytes 2097156 | tf_op jit(solution)/shard_map/while/body/eval_jaxpr/dynamic_update_slice | solution.py:100
  285.4 7.2 %copy.130 = f32[4,2,2,8,40,320]{5,4,2,1,0,3:T(8,128)} copy(f32[4,2,2,8,40,320]{5,4,3,2,1,0:T(8,128)} %bitcast.544) | data formatting | bytes 13107200 | tf_op jit(solution)/shard_map/reshape | solution.py:109
  292.6 50.1 %reduce-scatter.3.cloned.1.call-done = f32[96,256]{1,0:T(8,128)} async-done(((f32[3072,256]{1,0:T(8,128)}), f32[96,256]{1,0:T(8,128)}) %reduce-scatter.3.cloned.1.call-update) | async-done | bytes 98320 | tf_op jit(solution)/shard_map/reduce_scatter | solution.py:114
  342.8 127.5 %reduce-scatter.5.cloned.1.call-done = f32[1,2,2,40,320]{4,3,2,1,0:T(8,128)} async-done(((f32[32,2,2,40,320]{4,3,2,1,0:T(8,128)}), f32[1,2,2,40,320]{4,3,2,1,0:T(8,128)}) %reduce-scatter.5.cloned.1.call-update) | async-done | bytes 204816 | tf_op jit(solution)/shard_map/reduce_scatter | solution.py:113
  (150 shorter events, 40.2 us)
Async XLA Ops:
  7.2 1.6 copy-start.10
  7.2 65.5 %all-gather.3.cloned.1.call-start = ((), (), s32[]{:S(2)}) async-start(), calls=%async_computation.2 | async-start | bytes 3244032 | tf_op jit(solution)/shard_map/all_gather | solution.py:70
  7.9 120.5 %all-gather.5.cloned.1.call-start = ((), (), s32[]{:S(2)}) async-start(), calls=%async_computation.3 | async-start | bytes 9830400 | tf_op jit(solution)/shard_map/all_gather | solution.py:73
  8.7 3.2 copy-start.8
  8.7 334.1 %reduce-scatter.3.cloned.1.call-start = ((), (), s32[]{:S(2)}) async-start(), calls=%async_computation.4 | async-start | bytes 3244032 | tf_op jit(solution)/shard_map/reduce_scatter | solution.py:114
  139.1 6.5 %copy-start = (f32[2,6,256,256]{2,3,1,0:T(8,128)}, f32[2,6,256,256]{2,3,1,0:T(8,128)S(1)}, u32[]{:S(2)}) copy-start(f32[2,6,256,256]{2,3,1,0:T(8,128)S(1)} %get-tuple-element.426) | copy-start | bytes 9437188 | tf_op jit(solution)/shard_map/while
  145.6 1.5 copy-start.2
  149.5 1.0 copy-start.5
  149.5 1.0 copy-start.6
  154.7 1.0 copy-start.7
  178.5 1.1 copy-start.3
  178.5 1.1 copy-start.4
  182.5 5.4 %copy-start.1 = (f32[2,6,256,256]{2,3,1,0:T(8,128)S(1)}, f32[2,6,256,256]{2,3,1,0:T(8,128)}, u32[]{:S(2)}) copy-start(f32[2,6,256,256]{2,3,1,0:T(8,128)} %copy-done) | copy-start | bytes 9437188 | tf_op jit(solution)/shard_map/while
  187.8 6.5 %copy-start = (f32[2,6,256,256]{2,3,1,0:T(8,128)}, f32[2,6,256,256]{2,3,1,0:T(8,128)S(1)}, u32[]{:S(2)}) copy-start(f32[2,6,256,256]{2,3,1,0:T(8,128)S(1)} %get-tuple-element.426) | copy-start | bytes 9437188 | tf_op jit(solution)/shard_map/while
  194.3 1.5 copy-start.2
  198.3 1.0 copy-start.5
  198.3 1.0 copy-start.6
  203.4 1.0 copy-start.7
  227.2 1.1 copy-start.3
  227.3 1.1 copy-start.4
  231.2 6.3 %copy-start.1 = (f32[2,6,256,256]{2,3,1,0:T(8,128)S(1)}, f32[2,6,256,256]{2,3,1,0:T(8,128)}, u32[]{:S(2)}) copy-start(f32[2,6,256,256]{2,3,1,0:T(8,128)} %copy-done) | copy-start | bytes 9437188 | tf_op jit(solution)/shard_map/while
  241.1 229.2 %reduce-scatter.5.cloned.1.call-start = ((), (), s32[]{:S(2)}) async-start(), calls=%async_computation.5 | async-start | bytes 8110080 | tf_op jit(solution)/shard_map/reduce_scatter | solution.py:113
  241.1 4.0 copy-start.9
  241.1 4.0 copy-start.11
Sparse Core Ops, SparseCore 0:
  10.9 61.7 all-gather.2
  74.2 54.1 all-gather.4
  241.2 101.5 reduce-scatter.2
  348.8 121.3 reduce-scatter.4
where the time goes:
time: 479 us; the launch traced here: 477 us
  waiting for transfers between devices  293 us (61%)
  local copies, waits for them, and re-layouts  83.1 us (17%)
  other arithmetic  48.7 us (10%)
  matrix products  26.4 us (6%)
  between operations  13.9 us (3%)
  loops' own time  11.4 us (2%)
    reduce_scatter x1, waiting for transfers between devices, body(): lax.psum_scatter(arranged, ('scan', 'tile'), scatter_dimension=0, tiled=T...  128 us
    all_gather x1, waiting for transfers between devices, body(): lax.all_gather(probe_modes, ('scan', 'tile'), axis=0, tiled=True)  60.7 us
    all_gather x1, waiting for transfers between devices, body(): whole_object = lax.all_gather(object_tiles, 'tile', axis=0, tiled=True)  53.4 us
    reduce_scatter x1, waiting for transfers between devices, body(): lax.psum_scatter(probe_total.reshape(-1, pixels), ('scan', 'tile'), scatt...  50.1 us
    dynamic_update_slice x2, local copies, waits for them, and re-layouts, add_patch(): lax.dynamic_update_slice(object_total, current + gradient_piece[None], an...  22.7 us
    dot_general x32, matrix products, left_side(): jnp.einsum('ij,mjk->mik', matrix_part, component, preferred_element_type=...  13.3 us
    dot_general x32, matrix products, right_side(): jnp.einsum('mik,jk->mij', component, matrix_part, preferred_element_type=...  13.1 us
    mul x6, local copies, waits for them, and re-layouts, multiply_object(): real_part = exit_wave[0] * object_patch[0] - exit_wave[1] * object_patch[1]  13 us
  transfers between devices with their start and end apart: 4, of which 4 were waited for; matrix products, arithmetic and copies ran while one was open for 10% of the time, Pallas kernels for 0%

commit v1 on v0

v1 whole, which is shorter than its diff:
```python
import functools
import math

import jax
import jax.numpy as jnp
import ml_dtypes
import numpy as np
from jax import lax
from jax.experimental import pallas as pl
from jax.experimental.pallas import tpu as pltpu
from jax.sharding import PartitionSpec as P

MESH = pl.DeviceIdType.MESH
VMEM_BYTES = 56 * 1024 * 1024


def block_tables(pixels):
    index = np.arange(pixels, dtype=np.int64)
    offset = index[:, None] - index[None, :]
    chirp = (offset * offset % (2 * pixels)) * (math.pi / pixels)
    product = (index[:, None] * index[None, :] % pixels) * (2.0 * math.pi / pixels)
    scale = 1.0 / math.sqrt(pixels)
    tables = []
    for real, imag in ((np.cos(chirp), np.sin(chirp)), (np.cos(product), -np.sin(product))):
        real, imag = real * scale, imag * scale
        whole = np.block([[real, -imag], [imag, real]]).astype(np.float32)
        whole = whole.astype(ml_dtypes.bfloat16)
        tables += [whole, np.ascontiguousarray(whole.T)]
    return np.stack(tables)


def dot(left, right):
    return jnp.dot(left, right, preferred_element_type=jnp.float32)


def misfit_kernel(
    layers, group, tile_ref, corner_ref, probe_ref, object_ref, amplitude_ref, table_ref,
    probe_grad_ref, object_grad_ref, patch_ref, piece_ref, wave_ref, bright_ref,
):
    modes, pixels = probe_ref.shape[1], probe_ref.shape[2]
    positions = amplitude_ref.shape[0]
    planes, side = object_grad_ref.shape[0], object_grad_ref.shape[3]
    wide = -(-side // 128) * 128
    tall = min(pixels + 8, side)

    def clear(plane, carry):
        for tile in range(object_grad_ref.shape[1]):
            object_grad_ref[plane, tile] = jnp.zeros((side, side), jnp.float32)
        return carry

    lax.fori_loop(0, planes, clear, 0)

    def rows_of(value):
        return jnp.concatenate([value[:pixels], value[pixels:]], axis=1)

    def columns_of(value):
        return jnp.concatenate([value[:, :pixels], value[:, pixels:]], axis=0)

    def one_position(position, carry):
        tile = tile_ref[position]
        row, column = corner_ref[position, 0], corner_ref[position, 1]
        base = pl.multiple_of(jnp.minimum(row // 8 * 8, side - tall), 8)
        shift = row - base

        def cut(plane, carry):
            rows = object_ref[tile, plane, pl.ds(base, tall), :]
            padded = jnp.concatenate([rows, jnp.zeros((tall, wide - side), jnp.float32)], axis=1)
            moved = pltpu.roll(padded, lax.rem(wide - column, wide), 1)[:, :pixels]
            patch_ref[plane] = pltpu.roll(moved, lax.rem(tall - shift, tall), 0)[:pixels]
            piece_ref[plane] = jnp.zeros((pixels, pixels), jnp.float32)
            return carry

        lax.fori_loop(0, planes, cut, 0)
        bright_ref[...] = jnp.ones((pixels, pixels), jnp.float32)

        def incoming(layer, mode):
            if layer == 0:
                return probe_ref[0, mode], probe_ref[1, mode]
            return wave_ref[layer - 1, 0, mode], wave_ref[layer - 1, 1, mode]

        def table_at(layer):
            return 0 if layer < layers - 1 else 2

        def forward(step, carry):
            chosen = [step * group + member for member in range(group)]
            for layer in range(layers):
                at = table_at(layer)
                object_real, object_imag = patch_ref[2 * layer], patch_ref[2 * layer + 1]
                halves = []
                for mode in chosen:
                    real, imag = incoming(layer, mode)
                    rounded = jnp.concatenate(
                        [
                            real * object_real - imag * object_imag,
                            real * object_imag + imag * object_real,
                        ],
                        axis=0,
                    ).astype(jnp.bfloat16)
                    halves.append(dot(table_ref[at], rounded).astype(jnp.bfloat16))
                for mode, half in zip(chosen, halves):
                    wave = dot(rows_of(half), table_ref[at + 1])
                    real, imag = wave[:, :pixels], wave[:, pixels:]
                    wave_ref[layer, 0, mode] = real
                    wave_ref[layer, 1, mode] = imag
                    if layer == layers - 1:
                        bright_ref[...] += real * real + imag * imag
            return carry

        lax.fori_loop(0, modes // group, forward, 0)
        root = jnp.sqrt(bright_ref[...])
        measured = amplitude_ref[position].astype(jnp.float32)
        bright_ref[...] = 2.0 * (root - measured) / root

        def backward(step, carry):
            chosen = [step * group + member for member in range(group)]
            factor = bright_ref[...]
            cotangents = []
            for mode in chosen:
                real = wave_ref[layers - 1, 0, mode] * factor
                imag = wave_ref[layers - 1, 1, mode] * factor
                cotangents.append(jnp.concatenate([real, imag], axis=1).astype(jnp.bfloat16))
            for layer in reversed(range(layers)):
                at = table_at(layer)
                object_real, object_imag = patch_ref[2 * layer], patch_ref[2 * layer + 1]
                halves = [dot(value, table_ref[at]).astype(jnp.bfloat16) for value in cotangents]
                cotangents = []
                for mode, half in zip(chosen, halves):
                    change = dot(table_ref[at + 1], columns_of(half))
                    change = change.astype(jnp.bfloat16).astype(jnp.float32)
                    turn_real, turn_imag = change[:pixels], change[pixels:]
                    real, imag = incoming(layer, mode)
                    piece_ref[2 * layer] += turn_real * real + turn_imag * imag
                    piece_ref[2 * layer + 1] += turn_imag * real - turn_real * imag
                    back_real = turn_real * object_real + turn_imag * object_imag
                    back_imag = turn_imag * object_real - turn_real * object_imag
                    if layer > 0:
                        cotangents.append(
                            jnp.concatenate([back_real, back_imag], axis=1).astype(jnp.bfloat16)
                        )
                    else:
                        kept = position > 0
                        probe_grad_ref[0, mode] = back_real + jnp.where(
                            kept, probe_grad_ref[0, mode], 0.0
                        )
                        probe_grad_ref[1, mode] = back_imag + jnp.where(
                            kept, probe_grad_ref[1, mode], 0.0
                        )
            return carry

        lax.fori_loop(0, modes // group, backward, 0)

        def paste(plane, carry):
            padded = jnp.concatenate(
                [piece_ref[plane], jnp.zeros((tall - pixels, pixels), jnp.float32)], axis=0
            )
            moved = jnp.concatenate(
                [pltpu.roll(padded, shift, 0), jnp.zeros((tall, wide - pixels), jnp.float32)],
                axis=1,
            )
            moved = pltpu.roll(moved, column, 1)[:, :side]
            window = (plane, tile, pl.ds(base, tall), slice(None))
            object_grad_ref[window] = object_grad_ref[window] + moved
            return carry

        lax.fori_loop(0, planes, paste, 0)
        return carry

    lax.fori_loop(0, positions, one_position, 0)


def misfit_gradients(probe_field, whole_object, scan_offsets, patch_tiles, amplitudes):
    _, modes, pixels, _ = probe_field.shape
    tiles, planes, side, _ = whole_object.shape
    layers = planes // 2
    group = next(size for size in (3, 2, 1) if modes % size == 0)
    in_vmem = pl.BlockSpec(memory_space=pltpu.VMEM)
    in_smem = pl.BlockSpec(memory_space=pltpu.SMEM)
    return pl.pallas_call(
        functools.partial(misfit_kernel, layers, group),
        out_shape=(
            jax.ShapeDtypeStruct((2, modes, pixels, pixels), jnp.float32),
            jax.ShapeDtypeStruct((planes, tiles, side, side), jnp.float32),
        ),
        in_specs=[in_smem, in_smem, in_vmem, in_vmem, in_vmem, in_vmem],
        out_specs=(in_vmem, in_vmem),
        scratch_shapes=[
            pltpu.VMEM((planes, pixels, pixels), jnp.float32),
            pltpu.VMEM((planes, pixels, pixels), jnp.float32),
            pltpu.VMEM((layers, 2, modes, pixels, pixels), jnp.float32),
            pltpu.VMEM((pixels, pixels), jnp.float32),
        ],
        compiler_params=pltpu.CompilerParams(vmem_limit_bytes=VMEM_BYTES),
        name="misfit",
    )(
        patch_tiles, scan_offsets, probe_field, whole_object, amplitudes,
        jnp.asarray(block_tables(pixels)),
    )


class Cube:
    def __init__(self, scan_bits, tile_bits):
        scan, tile = lax.axis_index("scan"), lax.axis_index("tile")
        self.scan_names = ["s%d" % bit for bit in reversed(range(scan_bits))]
        self.tile_names = ["t%d" % bit for bit in reversed(range(tile_bits))]
        self.own, self.partner = {}, {}
        for axis, letter, index, bits in (("scan", "s", scan, scan_bits), ("tile", "t", tile, tile_bits)):
            for bit in range(bits):
                value = (index // (1 << bit)) % 2
                self.own[letter + str(bit)] = value
                self.partner[letter + str(bit)] = {axis: index + (1 - 2 * value) * (1 << bit)}

    def greet(self):
        barrier = pltpu.get_barrier_semaphore()
        for target in self.partner.values():
            pl.semaphore_signal(barrier, inc=1, device_id=target, device_id_type=MESH)
        pl.semaphore_wait(barrier, len(self.partner))


class Wires:
    def __init__(self, cube, send_sem, recv_sem):
        self.cube, self.send_sem, self.recv_sem, self.used = cube, send_sem, recv_sem, 0
        self.sent = []

    def start(self, source, target, name):
        copy = pltpu.make_async_remote_copy(
            src_ref=source,
            dst_ref=target,
            send_sem=self.send_sem.at[self.used],
            recv_sem=self.recv_sem.at[self.used],
            device_id=self.cube.partner[name],
            device_id_type=MESH,
        )
        self.used += 1
        copy.start()
        self.sent.append(copy)
        return copy

    def finish(self):
        for copy in self.sent:
            copy.wait_send()


def gather_kernel(
    scan_bits, tile_bits, probe_ref, object_ref, all_probe_ref, all_object_ref,
    send_sem, recv_sem, own_sem,
):
    cube = Cube(scan_bits, tile_bits)
    wires = Wires(cube, send_sem, recv_sem)
    own = cube.own
    names = cube.scan_names + cube.tile_names
    pixels = probe_ref.shape[1]
    planes = object_ref.shape[0]
    half = planes // 2
    across, beside = cube.tile_names[0], cube.tile_names[1]
    turn = cube.scan_names[-1]

    def probe_at(done, columns):
        bits = tuple(slice(None) if name in done else own[name] for name in names)
        return all_probe_ref.at[bits + (slice(None), columns)]

    def object_at(far, start, count):
        place = 1 - own[across] if far else own[across]
        return all_object_ref.at[place, own[beside], pl.ds(start, count)]

    halves = [pl.ds(0, pixels // 2), pl.ds(pixels // 2, pixels // 2)]
    early, late = cube.scan_names[:-1], cube.tile_names[-1:]
    orders = [early + [turn, across] + late, early + [across, turn] + late]

    cube.greet()
    own_probe = pltpu.make_async_copy(probe_ref, probe_at((), pl.ds(0, pixels)), own_sem.at[0])
    own_object = pltpu.make_async_copy(object_ref, object_at(False, 0, planes), own_sem.at[1])
    own_probe.start()
    own_object.start()

    def probe_step(step):
        copies = []
        for columns, order in zip(halves, orders):
            target = probe_at(order[:step], columns)
            source = probe_ref.at[:, columns] if step == 0 else target
            copies.append(wires.start(source, target, order[step]))
        return copies

    def settle(copies):
        for copy in copies:
            copy.wait_recv()

    moving = probe_step(0)
    first = own[turn] * half
    over = [
        wires.start(
            object_ref.at[pl.ds(first + j, 1)], object_at(False, first + j, 1), across
        )
        for j in range(half)
    ]
    near = [wires.start(object_ref, object_at(False, 0, planes), beside)]
    own_probe.wait()
    for step in range(1, len(early)):
        settle(moving)
        moving = probe_step(step)
    second = []
    for j in range(half):
        over[j].wait_recv()
        place = object_at(True, first + j, 1)
        second.append(wires.start(place, place, turn))
        near.append(wires.start(place, place, beside))
    settle(moving)
    moving = probe_step(len(early))
    other = (1 - own[turn]) * half
    for j in range(half):
        second[j].wait_recv()
        place = object_at(True, other + j, 1)
        near.append(wires.start(place, place, beside))
    for step in range(len(early) + 1, len(names)):
        settle(moving)
        moving = probe_step(step)
    settle(moving)
    settle(near)
    own_object.wait()
    wires.finish()


def gather(scan_bits, tile_bits, probe_modes, own_object):
    rows, pixels = probe_modes.shape
    planes, side, _ = own_object.shape
    bits = scan_bits + tile_bits
    copies = 2 * bits + 1 + 4 * (planes // 2)
    anywhere = pl.BlockSpec(memory_space=pl.ANY)
    return pl.pallas_call(
        functools.partial(gather_kernel, scan_bits, tile_bits),
        out_shape=(
            jax.ShapeDtypeStruct((2,) * bits + (rows, pixels), jnp.float32),
            jax.ShapeDtypeStruct((2,) * tile_bits + (planes, side, side), jnp.float32),
        ),
        in_specs=[anywhere, anywhere],
        out_specs=(anywhere, anywhere),
        scratch_shapes=[
            pltpu.SemaphoreType.DMA((copies,)),
            pltpu.SemaphoreType.DMA((copies,)),
            pltpu.SemaphoreType.DMA((2,)),
        ],
        compiler_params=pltpu.CompilerParams(
            collective_id=0, has_side_effects=True, vmem_limit_bytes=VMEM_BYTES
        ),
        name="gather",
    )(probe_modes, own_object)


def scatter_kernel(
    scan_bits, tile_bits, probe_ref, object_ref, probe_out_ref, object_out_ref,
    probe_land, object_land, send_sem, recv_sem,
):
    cube = Cube(scan_bits, tile_bits)
    wires = Wires(cube, send_sem, recv_sem)
    own = cube.own
    bits = scan_bits + tile_bits
    pixels = probe_out_ref.shape[1]
    halves, half = object_ref.shape[0], object_ref.shape[1]
    across, beside = cube.tile_names[0], cube.tile_names[1]
    turn = cube.scan_names[-1]
    rest = cube.scan_names[-2::-1]

    flows = []
    for j in range(half):
        for h in range(halves):
            middle = [across, turn] if h == 0 else [turn, across]
            order = [beside] + middle + rest
            lands = [land.at[h, j] for land in object_land]
            flows.append((order, cube.tile_names + cube.scan_names, object_ref, (h, j), (), lands, object_out_ref, (h, j)))
    for c in range(2):
        columns = pl.ds(c * (pixels // 2), pixels // 2)
        order = [beside] + (rest + [across, turn] if c == 0 else [across, turn] + rest)
        lands = [land.at[c] for land in probe_land]
        flows.append((order, cube.scan_names + cube.tile_names, probe_ref, (), (slice(None), columns), lands, probe_out_ref, (slice(None), columns)))

    def part(flow, step, kept):
        order, names, ref, front, back, lands, _, _ = flow
        names = [name for name in names if name not in order[:step]]
        place = tuple(
            (own[name] if kept else 1 - own[name]) if name == order[step] else slice(None)
            for name in names
        )
        if step == 0:
            return ref, front + place + (back if back else (slice(None), slice(None)))
        return lands[step - 1], place + (slice(None), slice(None))

    def send(flow, step):
        ref, place = part(flow, step, False)
        return wires.start(ref.at[place], flow[5][step], flow[0][step])

    cube.greet()
    moving = [send(flow, 0) for flow in flows]
    for step in range(bits):
        for number, flow in enumerate(flows):
            moving[number].wait_recv()
            ref, place = part(flow, step, True)
            land = flow[5][step]
            total = land[...] + ref[place]
            if step == bits - 1:
                flow[6][flow[7]] = total
            else:
                land[...] = total
                moving[number] = send(flow, step + 1)
    wires.finish()


def scatter(scan_bits, tile_bits, probe_total, object_total):
    rows, pixels = probe_total.shape[-2:]
    halves, half = object_total.shape[:2]
    tall, side = object_total.shape[-2:]
    bits = scan_bits + tile_bits
    copies = bits * (2 + halves * half)
    in_vmem = pl.BlockSpec(memory_space=pltpu.VMEM)
    return pl.pallas_call(
        functools.partial(scatter_kernel, scan_bits, tile_bits),
        out_shape=(
            jax.ShapeDtypeStruct((rows, pixels), jnp.float32),
            jax.ShapeDtypeStruct((halves, half, tall, side), jnp.float32),
        ),
        in_specs=[in_vmem, in_vmem],
        out_specs=(in_vmem, in_vmem),
        scratch_shapes=[
            [
                pltpu.VMEM((2,) + (2,) * (bits - 1 - step) + (rows, pixels // 2), jnp.float32)
                for step in range(bits)
            ],
            [
                pltpu.VMEM((halves, half) + (2,) * (bits - 1 - step) + (tall, side), jnp.float32)
                for step in range(bits)
            ],
            pltpu.SemaphoreType.DMA((copies,)),
            pltpu.SemaphoreType.DMA((copies,)),
        ],
        compiler_params=pltpu.CompilerParams(
            collective_id=1, has_side_effects=True, vmem_limit_bytes=VMEM_BYTES
        ),
        name="scatter",
    )(probe_total, object_total)


def body(probe_modes, object_tiles, scan_offsets, patch_tiles, amplitudes):
    tile_count = lax.axis_size("tile")
    scan_count = lax.axis_size("scan")
    rows, pixels = probe_modes.shape
    layers, side = object_tiles.shape[1], object_tiles.shape[3]
    planes = 2 * layers
    scan_bits, tile_bits = scan_count.bit_length() - 1, tile_count.bit_length() - 1
    assert scan_count == 1 << scan_bits and tile_count == 1 << tile_bits
    whole_probe, whole_object = gather(
        scan_bits, tile_bits, probe_modes, object_tiles.reshape(planes, side, side)
    )
    probe_total, object_total = misfit_gradients(
        whole_probe.reshape(2, -1, pixels, pixels),
        whole_object.reshape(tile_count, planes, side, side),
        scan_offsets,
        patch_tiles,
        amplitudes,
    )
    bits = (2,) * (scan_bits + tile_bits)
    probe_gradient, object_gradient = scatter(
        scan_bits,
        tile_bits,
        probe_total.reshape(bits + (rows, pixels)),
        object_total.reshape((2, layers) + bits + (side // scan_count, side)),
    )
    return (
        probe_gradient,
        object_gradient.reshape(1, layers, 2, side // scan_count, side),
    )


def solution(mesh):
    placed = (
        P(("scan", "tile"), None),
        P("tile", None, None, None, None),
        P(("scan", "tile"), None),
        P(("scan", "tile")),
        P(("scan", "tile"), None, None),
    )
    return jax.shard_map(
        body,
        mesh=mesh,
        in_specs=placed,
        out_specs=(P(("scan", "tile"), None), P("tile", None, None, "scan", None)),
        check_vma=False,
    )
```

time: 479 us -> 171 us (0.36)
  waiting for transfers between devices: 293 us -> 0 us
  Pallas kernels: 0 us -> 167 us
  local copies, waits for them, and re-layouts: 83.1 us -> 3.19 us
  other arithmetic: 48.7 us -> 0 us
  matrix products: 26.4 us -> 0 us
  between operations: 13.9 us -> 0.65 us
  loops' own time: 11.4 us -> 0 us
    reduce_scatter x2 -> x0, waiting for transfers between devices: 178 us -> none  [the longest x1 128 us: body(): lax.psum_scatter(arranged, ('scan', 'tile'), scatter_dimension=0, tiled=T...]
    pallas_call x0 -> x3, Pallas kernels: none -> 167 us  [the longest x1 68.1 us: gather(): pl.pallas_call(functools.partial(gather_kernel, scan_bits, tile_bits), ou...]
    all_gather x2 -> x0, waiting for transfers between devices: 114 us -> none  [the longest x1 60.7 us: body(): lax.all_gather(probe_modes, ('scan', 'tile'), axis=0, tiled=True)]
    dot_general x64 -> x0, matrix products: 26.4 us -> none  [the longest x32 13.3 us: left_side(): jnp.einsum('ij,mjk->mik', matrix_part, component, preferred_element_type=...]
    dynamic_update_slice x2 -> x0, local copies, waits for them, and re-layouts: 22.7 us -> none  [add_patch(): lax.dynamic_update_slice(object_total, current + gradient_piece[None], an...]
    add x4 -> x0, other arithmetic: 15.9 us -> none  [the longest x2 11.6 us: one_position(): return (probe_total + probe_part, patch_part)]
    reduce_sum x8 -> x0, local copies, waits for them, and re-layouts: 14.3 us -> none  [the longest x4 7.13 us: multiply_object(): real_part = exit_wave[0] * object_patch[0] - exit_wave[1] * object_patch[1]]
    mul x6 -> x0, local copies, waits for them, and re-layouts: 13 us -> none  [multiply_object(): real_part = exit_wave[0] * object_patch[0] - exit_wave[1] * object_patch[1]]
  transfers between devices with their start and end apart: 4 -> 0, of which waited for: 4 -> 0; matrix products, arithmetic and copies ran while one was open for 10% -> 0% of each run, Pallas kernels for 0% -> 0%
where the time goes in v1:
time: 171 us
  Pallas kernels  167 us (98%)
  local copies, waits for them, and re-layouts  3.19 us (2%)
    pallas_call x1, Pallas kernels, gather(): pl.pallas_call(functools.partial(gather_kernel, scan_bits, tile_bits), ou...  68.1 us
    pallas_call x1, Pallas kernels, scatter(): pl.pallas_call(functools.partial(scatter_kernel, scan_bits, tile_bits), o...  67.8 us
    pallas_call x1, Pallas kernels, misfit_gradients(): pl.pallas_call(functools.partial(misfit_kernel, layers, group), out_shape...  31.5 us

profile of v1, /device:TPU:0, one launch (start us, length us, event | category | flops | bytes accessed | tf_op | source)
XLA Modules:
  0.0 171.3 jit_solution(4551040944168153369)
XLA Ops:
  0.6 68.1 %gather.1 = (f32[2,2,2,2,2,96,256]{6,5,4,3,2,1,0:T(8,128)}, f32[2,2,4,320,320]{4,3,2,1,0:T(8,128)}) custom-call(f32[96,256]{1,0:T(8,128)} %probe_ref.1, f32[4,320,320]{2,1,0:T(8,128)} %bitcast.10), custom_call_target="tpu_custom_call" | custom-call | tf_op jit(solution)/shard_map/gather/pallas_call | solution.py:328
  68.8 31.5 %misfit.1 = (f32[2,6,256,256]{3,2,1,0:T(8,128)}, f32[4,4,320,320]{3,2,1,0:T(8,128)}) custom-call(s32[2]{0:T(128)} %tile_ref.1, s32[2,2]{1,0:T(2,128)} %corner_ref.1, f32[2,6,256,256]{3,2,1,0:T(8,128)} %bitcast.9, f32[4,4,320,320]{3,2,1,0:T(8,128)} %bitcast.7, bf16[2,256,256]{2,1,0:T(8,128)(2,1)} %amplitude_ref.1, bf16[4,512,512]{2,1,0:T(8,128)(2,1)} %constant.2.clone.table_ref), custom_call_target="tpu_custom_call" | custom-call | tf_op jit(solution)/shard_map/misfit/pallas_call | solution.py:178
  100.3 67.8 %scatter.1 = (f32[96,256]{1,0:T(8,128)}, f32[2,2,40,320]{3,2,1,0:T(8,128)}) custom-call(f32[2,2,2,2,2,96,256]{6,5,4,3,2,1,0:T(8,128)} %bitcast.8, f32[2,2,2,2,2,2,2,40,320]{8,7,6,5,4,3,2,1,0:T(8,128)} %bitcast.6), custom_call_target="tpu_custom_call" | custom-call | tf_op jit(solution)/shard_map/scatter/pallas_call | solution.py:413
  168.1 1.5 copy.10
  169.6 1.7 copy.11

commit v2 on v1

--- a/solution.py
+++ b/solution.py
@@ -197,6 +197,16 @@
     )
 
 
+def two_parts(rows, pixels):
+    if rows % 16 == 0:
+        return [(pl.ds(c * (rows // 2), rows // 2), slice(None)) for c in range(2)]
+    return [(slice(None), pl.ds(c * (pixels // 2), pixels // 2)) for c in range(2)]
+
+
+def part_shape(rows, pixels):
+    return (rows // 2, pixels) if rows % 16 == 0 else (rows, pixels // 2)
+
+
 class Cube:
     def __init__(self, scan_bits, tile_bits):
         scan, tile = lax.axis_index("scan"), lax.axis_index("tile")
@@ -248,35 +258,34 @@
     wires = Wires(cube, send_sem, recv_sem)
     own = cube.own
     names = cube.scan_names + cube.tile_names
-    pixels = probe_ref.shape[1]
     planes = object_ref.shape[0]
     half = planes // 2
     across, beside = cube.tile_names[0], cube.tile_names[1]
     turn = cube.scan_names[-1]
 
-    def probe_at(done, columns):
+    def probe_at(done, place):
         bits = tuple(slice(None) if name in done else own[name] for name in names)
-        return all_probe_ref.at[bits + (slice(None), columns)]
+        return all_probe_ref.at[bits + place]
 
     def object_at(far, start, count):
         place = 1 - own[across] if far else own[across]
         return all_object_ref.at[place, own[beside], pl.ds(start, count)]
 
-    halves = [pl.ds(0, pixels // 2), pl.ds(pixels // 2, pixels // 2)]
+    halves = two_parts(*probe_ref.shape)
     early, late = cube.scan_names[:-1], cube.tile_names[-1:]
     orders = [early + [turn, across] + late, early + [across, turn] + late]
 
     cube.greet()
-    own_probe = pltpu.make_async_copy(probe_ref, probe_at((), pl.ds(0, pixels)), own_sem.at[0])
+    own_probe = pltpu.make_async_copy(probe_ref, probe_at((), (slice(None), slice(None))), own_sem.at[0])
     own_object = pltpu.make_async_copy(object_ref, object_at(False, 0, planes), own_sem.at[1])
     own_probe.start()
     own_object.start()
 
     def probe_step(step):
         copies = []
-        for columns, order in zip(halves, orders):
-            target = probe_at(order[:step], columns)
-            source = probe_ref.at[:, columns] if step == 0 else target
+        for place, order in zip(halves, orders):
+            target = probe_at(order[:step], place)
+            source = probe_ref.at[place] if step == 0 else target
             copies.append(wires.start(source, target, order[step]))
         return copies
 
@@ -353,7 +362,6 @@
     wires = Wires(cube, send_sem, recv_sem)
     own = cube.own
     bits = scan_bits + tile_bits
-    pixels = probe_out_ref.shape[1]
     halves, half = object_ref.shape[0], object_ref.shape[1]
     across, beside = cube.tile_names[0], cube.tile_names[1]
     turn = cube.scan_names[-1]
@@ -366,11 +374,10 @@
             order = [beside] + middle + rest
             lands = [land.at[h, j] for land in object_land]
             flows.append((order, cube.tile_names + cube.scan_names, object_ref, (h, j), (), lands, object_out_ref, (h, j)))
-    for c in range(2):
-        columns = pl.ds(c * (pixels // 2), pixels // 2)
+    for c, block in enumerate(two_parts(*probe_out_ref.shape)):
         order = [beside] + (rest + [across, turn] if c == 0 else [across, turn] + rest)
         lands = [land.at[c] for land in probe_land]
-        flows.append((order, cube.scan_names + cube.tile_names, probe_ref, (), (slice(None), columns), lands, probe_out_ref, (slice(None), columns)))
+        flows.append((order, cube.scan_names + cube.tile_names, probe_ref, (), block, lands, probe_out_ref, block))
 
     def part(flow, step, kept):
         order, names, ref, front, back, lands, _, _ = flow
@@ -420,7 +427,7 @@
         out_specs=(in_vmem, in_vmem),
         scratch_shapes=[
             [
-                pltpu.VMEM((2,) + (2,) * (bits - 1 - step) + (rows, pixels // 2), jnp.float32)
+                pltpu.VMEM((2,) + (2,) * (bits - 1 - step) + part_shape(rows, pixels), jnp.float32)
                 for step in range(bits)
             ],
             [

time: 171 us -> 172 us (level)
  no operation moved by 1% of the time
where the time goes in v2:
time: 172 us; the launch traced here: 171 us
  Pallas kernels  168 us (98%)
  local copies, waits for them, and re-layouts  3.19 us (2%)
    pallas_call x1, Pallas kernels, gather(): pl.pallas_call(functools.partial(gather_kernel, scan_bits, tile_bits), ou...  68.1 us
    pallas_call x1, Pallas kernels, scatter(): pl.pallas_call(functools.partial(scatter_kernel, scan_bits, tile_bits), o...  67.9 us
    pallas_call x1, Pallas kernels, misfit_gradients(): pl.pallas_call(functools.partial(misfit_kernel, layers, group), out_shape...  31.5 us

profile of v2, /device:TPU:0, one launch (start us, length us, event | category | flops | bytes accessed | tf_op | source)
XLA Modules:
  0.0 171.4 jit_solution(12463481168756365522)
XLA Ops:
  0.6 68.1 %gather.1 = (f32[2,2,2,2,2,96,256]{6,5,4,3,2,1,0:T(8,128)}, f32[2,2,4,320,320]{4,3,2,1,0:T(8,128)}) custom-call(f32[96,256]{1,0:T(8,128)} %probe_ref.1, f32[4,320,320]{2,1,0:T(8,128)} %bitcast.10), custom_call_target="tpu_custom_call" | custom-call | tf_op jit(solution)/shard_map/gather/pallas_call | solution.py:337
  68.8 31.5 %misfit.1 = (f32[2,6,256,256]{3,2,1,0:T(8,128)}, f32[4,4,320,320]{3,2,1,0:T(8,128)}) custom-call(s32[2]{0:T(128)} %tile_ref.1, s32[2,2]{1,0:T(2,128)} %corner_ref.1, f32[2,6,256,256]{3,2,1,0:T(8,128)} %bitcast.9, f32[4,4,320,320]{3,2,1,0:T(8,128)} %bitcast.7, bf16[2,256,256]{2,1,0:T(8,128)(2,1)} %amplitude_ref.1, bf16[4,512,512]{2,1,0:T(8,128)(2,1)} %constant.2.clone.table_ref), custom_call_target="tpu_custom_call" | custom-call | tf_op jit(solution)/shard_map/misfit/pallas_call | solution.py:178
  100.2 67.9 %scatter.1 = (f32[96,256]{1,0:T(8,128)}, f32[2,2,40,320]{3,2,1,0:T(8,128)}) custom-call(f32[2,2,2,2,2,96,256]{6,5,4,3,2,1,0:T(8,128)} %bitcast.8, f32[2,2,2,2,2,2,2,40,320]{8,7,6,5,4,3,2,1,0:T(8,128)} %bitcast.6), custom_call_target="tpu_custom_call" | custom-call | tf_op jit(solution)/shard_map/scatter/pallas_call | solution.py:420
  168.2 1.5 copy.10
  169.7 1.7 copy.11
